TPU v7x, 256 devices: a whole 4x4x8 slice. The times are simulated.
256 devices in a mesh: pp: 4 (over x_lo, core), dp: 16 (over z, x_hi), tp: 4 (over y).
Axes of the slice: x: 4 (x_hi: 2, x_lo: 2; x = x_hi * 2 + x_lo), y: 4, z: 8, core: 2. Of those that a mesh axis runs over, the one named last changes fastest.
Arguments:
- activations: bfloat16 [4, 2, 2048, 2048], P('pp', None, 'dp'), may hold values from -6 to 6
- upstream_grad: bfloat16 [2, 2048, 2048], P(None, 'dp'), may hold values from -6 to 6
- norm_gain: float32 [4, 2048], P('pp'), may hold values from 0.1 to 1.9
- value_weight: bfloat16 [4, 2048, 2048], P('pp', None, 'tp'), may hold values from -0.125 to 0.125
- gate_weight: bfloat16 [4, 2048, 2048], P('pp', None, 'tp'), may hold values from -0.125 to 0.125
- out_weight: bfloat16 [4, 2048, 2048], P('pp', 'tp'), may hold values from -0.125 to 0.125
- conv_weight: float32 [4, 4, 2048], P('pp', None, 'tp'), may hold values from -3 to 3
Outputs:
- input_grads: bfloat16 [4, 2, 2048, 2048], P('pp', None, ('dp', 'tp'))
- value_grad: float32 [4, 2048, 2048], P('pp', 'dp', 'tp')
- gate_grad: float32 [4, 2048, 2048], P('pp', 'dp', 'tp')
- out_grad: float32 [4, 2048, 2048], P('pp', 'dp', 'tp')
All inputs are finite; a program needn't handle non-finite values.
Results may differ from a plain program's by a relative error of at most 0.02.
Values may be sent and summed in bfloat16 or wider, within the bound.
No kernel may reach another device: no remote copies, remote signals or barrier semaphores. Data moves between devices by JAX's collectives and lax.ppermute only.
A program may use at most 128 MiB of HBM per device.

v0:
```python
import jax
import jax.numpy as jnp
from jax import lax
from jax.sharding import PartitionSpec as P

EPSILON = 1e-06


def from_behind(shard, axis, by):
    length = lax.axis_size(axis)
    pairs = [(i, i + by) for i in range(length) if 0 <= i + by < length]
    return lax.ppermute(shard, axis, pairs)


def causal_conv(values, kernel):
    width = kernel.shape[0]
    length = values.shape[0]
    padded = jnp.pad(values, ((width - 1, 0), (0, 0)))
    total = jnp.zeros_like(values)
    for offset in range(width):
        begin = width - 1 - offset
        total = total + kernel[offset] * lax.slice_in_dim(padded, begin, begin + length, axis=0)
    return total


def conv_adjoint(grads, kernel):
    width = kernel.shape[0]
    length = grads.shape[0]
    padded = jnp.pad(grads, ((0, width - 1), (0, 0)))
    total = jnp.zeros_like(grads)
    for offset in range(width):
        total = total + kernel[offset] * lax.slice_in_dim(padded, offset, offset + length, axis=0)
    return total


def local_back(inputs, upstream, gain, value_w, gate_w, out_w, kernel):
    floats = inputs.astype(jnp.float32)
    inv_rms = lax.rsqrt(jnp.mean(floats * floats, axis=-1, keepdims=True) + EPSILON)
    unit = floats * inv_rms
    normed = (unit * gain).astype(jnp.bfloat16)
    values = jnp.dot(normed, value_w, preferred_element_type=jnp.float32)
    gate_logit = jnp.dot(normed, gate_w, preferred_element_type=jnp.float32)
    mixed = causal_conv(values, kernel)
    sig_mix = jax.nn.sigmoid(mixed)
    act = mixed * sig_mix
    gate = jax.nn.sigmoid(gate_logit)
    hidden = (act * gate).astype(jnp.bfloat16)
    d_hidden = jnp.dot(upstream, out_w.T, preferred_element_type=jnp.float32)
    d_gate = (d_hidden * act * gate * (1.0 - gate)).astype(jnp.bfloat16)
    d_mixed = d_hidden * gate * sig_mix * (1.0 + mixed * (1.0 - sig_mix))
    d_values = conv_adjoint(d_mixed, kernel).astype(jnp.bfloat16)
    return (normed, unit, inv_rms, hidden, d_values, d_gate)


def weight_terms(totals, normed, upstream, hidden, d_values, d_gate):
    return (
        totals[0] + jnp.dot(normed.T, d_values, preferred_element_type=jnp.float32),
        totals[1] + jnp.dot(normed.T, d_gate, preferred_element_type=jnp.float32),
        totals[2] + jnp.dot(upstream.T, hidden, preferred_element_type=jnp.float32),
    )


def shards(
    activations, upstream_grad, norm_gain, value_weight, gate_weight, out_weight, conv_weight
):
    stored = activations[0]
    gain = norm_gain[0]
    value_w = value_weight[0]
    gate_w = gate_weight[0]
    out_w = out_weight[0]
    kernel = conv_weight[0]
    sections = lax.axis_size("pp")
    section_id = lax.axis_index("pp")
    tp_count = lax.axis_size("tp")
    tp_index = lax.axis_index("tp")
    micro_count = stored.shape[0]
    length = stored.shape[1]
    width = stored.shape[2]
    channels = value_w.shape[1]
    share = length // tp_count
    row_start = tp_index * share
    factor = (micro_count * length * lax.axis_size("dp")) ** (-0.5)
    is_last = section_id == sections - 1
    slots = micro_count + 1

    def zero_back(inputs, upstream):
        return (
            jnp.zeros((length, width), jnp.bfloat16),
            jnp.zeros((length, width), jnp.float32),
            jnp.zeros((length, 1), jnp.float32),
            jnp.zeros((length, channels), jnp.bfloat16),
            jnp.zeros((length, channels), jnp.bfloat16),
            jnp.zeros((length, channels), jnp.bfloat16),
        )

    def real_back(inputs, upstream):
        return local_back(inputs, upstream, gain, value_w, gate_w, out_w, kernel)

    zero_grad = jnp.zeros((width, channels), jnp.float32)
    totals = (zero_grad, zero_grad, zero_grad)
    saved_normed = jnp.zeros((slots, length, width), jnp.bfloat16)
    saved_upstream = jnp.zeros((slots, length, width), jnp.bfloat16)
    saved_hidden = jnp.zeros((slots, length, channels), jnp.bfloat16)
    saved_values = jnp.zeros((slots, length, channels), jnp.bfloat16)
    saved_gate = jnp.zeros((slots, length, channels), jnp.bfloat16)
    grads_out = jnp.zeros((slots, share, width), jnp.bfloat16)
    incoming = jnp.zeros((length, width), jnp.bfloat16)
    ticks = sections + micro_count - 1
    for tick in range(ticks):
        position = tick - (sections - 1 - section_id)
        valid = (position >= 0) & (position < micro_count)
        clipped = jnp.clip(position, 0, micro_count - 1)
        target = jnp.where(valid, clipped, micro_count)
        own_inputs = lax.dynamic_index_in_dim(stored, clipped, 0, keepdims=False)
        arriving = lax.dynamic_index_in_dim(upstream_grad, clipped, 0, keepdims=False)
        received = incoming
        upstream = jnp.where(is_last, arriving, received)
        normed, unit, inv_rms, hidden, d_values, d_gate = lax.cond(
            valid, real_back, zero_back, own_inputs, upstream
        )
        d_normed = lax.psum_scatter(
            jnp.dot(d_values, value_w.T, preferred_element_type=jnp.float32)
            + jnp.dot(d_gate, gate_w.T, preferred_element_type=jnp.float32),
            "tp",
            scatter_dimension=0,
            tiled=True,
        )
        unit_rows = lax.dynamic_slice_in_dim(unit, row_start, share, 0)
        inv_rows = lax.dynamic_slice_in_dim(inv_rms, row_start, share, 0)
        upstream_rows = lax.dynamic_slice_in_dim(upstream, row_start, share, 0)
        d_unit = d_normed * gain
        d_share = (
            upstream_rows.astype(jnp.float32)
            + inv_rows * (d_unit - unit_rows * jnp.mean(d_unit * unit_rows, axis=-1, keepdims=True))
        ).astype(jnp.bfloat16)
        grads_out = lax.dynamic_update_index_in_dim(grads_out, d_share, target, 0)
        saved_normed = lax.dynamic_update_index_in_dim(saved_normed, normed, target, 0)
        saved_upstream = lax.dynamic_update_index_in_dim(saved_upstream, upstream, target, 0)
        saved_hidden = lax.dynamic_update_index_in_dim(saved_hidden, hidden, target, 0)
        saved_values = lax.dynamic_update_index_in_dim(saved_values, d_values, target, 0)
        saved_gate = lax.dynamic_update_index_in_dim(saved_gate, d_gate, target, 0)
        if tick < ticks - 1:
            whole_grad = lax.all_gather(d_share, "tp", axis=0, tiled=True)
            incoming = from_behind(whole_grad, "pp", -1)
    for micro_index in range(micro_count):
        totals = weight_terms(
            totals,
            saved_normed[micro_index],
            saved_upstream[micro_index],
            saved_hidden[micro_index],
            saved_values[micro_index],
            saved_gate[micro_index],
        )
    summed_value, summed_gate, summed_out = (
        lax.psum_scatter(
            totals[0].astype(jnp.bfloat16), "dp", scatter_dimension=0, tiled=True
        ).astype(jnp.float32),
        lax.psum_scatter(
            totals[1].astype(jnp.bfloat16), "dp", scatter_dimension=0, tiled=True
        ).astype(jnp.float32),
        lax.psum_scatter(
            totals[2].astype(jnp.bfloat16), "dp", scatter_dimension=0, tiled=True
        ).astype(jnp.float32),
    )
    return (
        grads_out[:micro_count][None],
        (summed_value * factor)[None],
        (summed_gate * factor)[None],
        (summed_out * factor)[None],
    )


def solution(mesh):
    placed = (
        P("pp", None, "dp", None),
        P(None, "dp", None),
        P("pp", None),
        P("pp", None, "tp"),
        P("pp", None, "tp"),
        P("pp", "tp", None),
        P("pp", None, "tp"),
    )
    return jax.shard_map(
        shards,
        mesh=mesh,
        in_specs=placed,
        out_specs=(
            P("pp", None, ("dp", "tp"), None),
            P("pp", "dp", "tp"),
            P("pp", "dp", "tp"),
            P("pp", "dp", "tp"),
        ),
        check_vma=False,
    )
```

profile of v0, /device:TPU:8, one launch (start us, length us, event | category | flops | bytes accessed | tf_op | source)
XLA Modules:
  0.0 972.6 jit_solution(5823771275020703180)
XLA Ops:
  7.5 2.2 constant_dynamic-update-slice_fusion.4
  9.6 1.2 copy-done.17
  10.8 1.9 conditional.5
  13.5 2.5 fusion.102
  16.1 2.8 convolution_add_fusion.4
  19.5 33.1 %reduce-scatter.9.cloned.1.call-done = f32[32,2048]{1,0:T(8,128)} async-done(((f32[128,2048]{1,0:T(8,128)}), f32[32,2048]{1,0:T(8,128)}) %reduce-scatter.9.cloned.1.call-update) | async-done | bytes 262160 | tf_op jit(solution)/shard_map/reduce_scatter | solution.py:121
  52.6 1.2 multiply_reduce_fusion.4
  53.8 1.2 bitcast_dynamic-update-slice_fusion.7
  55.0 14.2 %all_gather.12 = bf16[128,2048]{1,0:T(8,128)(2,1)} all-gather(bf16[32,2048]{1,0:T(8,128)(2,1)S(1)} %get-tuple-element.347), channel_id=1, replica_groups=mesh['pp'=4,'dp'=16,'tp'=4] {'tp'}, dimensions={0}, use_global_device_ids=true | all-gather | bytes 655360 | tf_op jit(solution)/shard_map/all_gather | solution.py:143
  69.2 1.3 collective-permute-start
  70.5 2.8 collective-permute-done
  73.4 2.4 bitcast_dynamic-update-slice_fusion.3
  75.7 3.7 conditional.6
  80.8 1.8 fusion.110
  82.7 2.8 convolution_add_fusion.3
  86.6 35.9 %reduce-scatter.11.cloned.1.call-done = f32[32,2048]{1,0:T(8,128)} async-done(((f32[128,2048]{1,0:T(8,128)}), f32[32,2048]{1,0:T(8,128)}) %reduce-scatter.11.cloned.1.call-update) | async-done | bytes 262160 | tf_op jit(solution)/shard_map/reduce_scatter | solution.py:121
  123.7 1.2 bitcast_dynamic-update-slice_fusion.6
  124.9 13.9 %all_gather.13 = bf16[128,2048]{1,0:T(8,128)(2,1)} all-gather(bf16[32,2048]{1,0:T(8,128)(2,1)S(1)} %get-tuple-element.345), channel_id=1, replica_groups=mesh['pp'=4,'dp'=16,'tp'=4] {'tp'}, dimensions={0}, use_global_device_ids=true | all-gather | bytes 655360 | tf_op jit(solution)/shard_map/all_gather | solution.py:143
  138.8 1.3 collective-permute-start.1
  140.1 2.8 collective-permute-done.1
  142.9 2.4 bitcast_dynamic-update-slice_fusion.2
  145.3 3.2 conditional.7
  150.5 1.8 fusion.108
  152.4 2.8 convolution_add_fusion.2
  155.4 1.3 fusion.95
  156.6 37.2 %reduce-scatter.13.cloned.1.call-done = f32[32,2048]{1,0:T(8,128)} async-done(((f32[128,2048]{1,0:T(8,128)}), f32[32,2048]{1,0:T(8,128)}) %reduce-scatter.13.cloned.1.call-update) | async-done | bytes 262160 | tf_op jit(solution)/shard_map/reduce_scatter | solution.py:121
  195.0 1.2 bitcast_dynamic-update-slice_fusion.5
  196.2 14.2 %all_gather.14 = bf16[128,2048]{1,0:T(8,128)(2,1)} all-gather(bf16[32,2048]{1,0:T(8,128)(2,1)S(1)} %get-tuple-element.343), channel_id=1, replica_groups=mesh['pp'=4,'dp'=16,'tp'=4] {'tp'}, dimensions={0}, use_global_device_ids=true | all-gather | bytes 655360 | tf_op jit(solution)/shard_map/all_gather | solution.py:143
  210.4 1.3 collective-permute-start.2
  211.7 2.8 collective-permute-done.2
  214.5 2.4 bitcast_dynamic-update-slice_fusion.1
  216.9 10.8 %conditional.8 = (f32[128,2048]{1,0:T(8,128)}, f32[128,1]{0,1:T(1,128)}, bf16[128,512]{1,0:T(8,128)(2,1)S(1)}, bf16[128,512]{1,0:T(8,128)(2,1)}, bf16[1,128,2048...) conditional(s32[]{:T(128)} %convert_element_type.299, ...), branch_computations={%region_15.16_spmd, %region_16.18_spmd} | conditional | flops 811794560 | bytes 23923816 | solution.py:118
  219.0 1.7 fusion.57
  220.7 1.8 fusion.67
  223.4 2.6 multiply_convert_fusion.17
  229.2 1.8 fusion.106
  231.0 2.8 convolution_add_fusion.1
  235.0 30.1 %reduce-scatter.15.cloned.1.call-done = f32[32,2048]{1,0:T(8,128)} async-done(((f32[128,2048]{1,0:T(8,128)}), f32[32,2048]{1,0:T(8,128)}) %reduce-scatter.15.cloned.1.call-update) | async-done | bytes 262160 | tf_op jit(solution)/shard_map/reduce_scatter | solution.py:121
  265.1 1.2 multiply_reduce_fusion.1
  266.3 1.2 bitcast_dynamic-update-slice_fusion.4
  267.5 13.9 %all_gather.15 = bf16[128,2048]{1,0:T(8,128)(2,1)} all-gather(bf16[32,2048]{1,0:T(8,128)(2,1)S(1)} %get-tuple-element.341), channel_id=1, replica_groups=mesh['pp'=4,'dp'=16,'tp'=4] {'tp'}, dimensions={0}, use_global_device_ids=true | all-gather | bytes 655360 | tf_op jit(solution)/shard_map/all_gather | solution.py:143
  281.4 1.3 collective-permute-start.3
  283.6 1.6 constant_dynamic-update-slice_fusion.9
  285.5 1.2 constant_dynamic-update-slice_fusion.2
  286.7 2.2 bitcast_dynamic-update-slice_fusion
  289.0 9.8 %conditional.9 = (f32[128,2048]{1,0:T(8,128)}, f32[128,1]{0,1:T(1,128)}, bf16[128,512]{1,0:T(8,128)(2,1)}, bf16[128,512]{1,0:T(8,128)(2,1)}, bf16[1,128,2048]{2,...) conditional(s32[]{:T(128)} %convert_element_type.302, ...), branch_computations={%region_20.21_spmd, %region_21.23_spmd} | conditional | flops 811794560 | bytes 28118148 | solution.py:118
  293.0 2.6 multiply_convert_fusion.22
  295.6 1.6 copy.99
  298.7 1.9 fusion.104
  300.6 2.9 convolution_add_fusion
  303.5 1.7 constant_dynamic-update-slice_fusion.8
  305.3 1.6 constant_dynamic-update-slice_fusion.1
  307.7 1.6 constant_dynamic-update-slice_fusion.5
  310.4 1.6 fusion.88
  312.0 3.0 add_convert_fusion.6
  320.4 2.1 add_convert_fusion.7
  325.3 2.1 add_convert_fusion.5
  328.3 2.0 reduce-scatter.17.cloned.1.call-done
  333.2 210.7 %reduce-scatter.21.cloned.1.call-done = bf16[128,512]{1,0:T(8,128)(2,1)} async-done(((bf16[2048,512]{1,0:T(8,128)(2,1)}), bf16[128,512]{1,0:T(8,128)(2,1)}) %reduce-scatter.21.cloned.1.call-update) | async-done | bytes 131088 | tf_op jit(solution)/shard_map/reduce_scatter | solution.py:158
  544.0 1.6 multiply_bitcast_fusion.1
  545.6 208.5 %reduce-scatter.19.cloned.1.call-done = bf16[128,512]{1,0:T(8,128)(2,1)} async-done(((bf16[2048,512]{1,0:T(8,128)(2,1)}), bf16[128,512]{1,0:T(8,128)(2,1)}) %reduce-scatter.19.cloned.1.call-update) | async-done | bytes 131088 | tf_op jit(solution)/shard_map/reduce_scatter | solution.py:155
  754.1 1.6 multiply_bitcast_fusion.2
  755.7 208.4 %reduce-scatter.23.cloned.1.call-done = bf16[128,512]{1,0:T(8,128)(2,1)} async-done(((bf16[2048,512]{1,0:T(8,128)(2,1)}), bf16[128,512]{1,0:T(8,128)(2,1)}) %reduce-scatter.23.cloned.1.call-update) | async-done | bytes 131088 | tf_op jit(solution)/shard_map/reduce_scatter | solution.py:161
  964.2 1.6 multiply_bitcast_fusion
  (183 shorter events, 45.6 us)
Async XLA Ops:
  7.2 2.4 copy-start.16
  7.2 2.4 copy-start
  7.2 2.4 copy-start.10
  7.2 2.4 copy-start.41
  7.2 45.4 %reduce-scatter.9.cloned.1.call-start = ((), (), s32[]{:S(2)}) async-start(), calls=%async_computation.8 | async-start | bytes 1310720 | tf_op jit(solution)/shard_map/reduce_scatter | solution.py:121
  9.6 1.2 copy-start.17
  12.7 0.8 copy-start.19
  13.5 2.5 copy-start.33
  13.5 2.6 copy-start.34
  13.5 2.6 copy-start.36
  18.9 103.6 %reduce-scatter.11.cloned.1.call-start = ((), (), s32[]{:S(2)}) async-start(), calls=%async_computation.9 | async-start | bytes 1310720 | tf_op jit(solution)/shard_map/reduce_scatter | solution.py:121
  69.2 4.1 collective-permute-start
  70.5 5.2 copy-start.1
  79.4 0.8 copy-start.21
  80.2 0.7 copy-start.29
  80.2 2.4 copy-start.38
  80.2 2.4 copy-start.2
  85.4 108.4 %reduce-scatter.13.cloned.1.call-start = ((), (), s32[]{:S(2)}) async-start(), calls=%async_computation.10 | async-start | bytes 1310720 | tf_op jit(solution)/shard_map/reduce_scatter | solution.py:121
  138.8 4.1 collective-permute-start.1
  140.1 5.2 copy-start.3
  148.5 0.8 copy-start.23
  149.3 0.6 copy-start.47
  149.9 0.6 copy-start.30
  149.9 2.4 copy-start.31
  149.9 2.4 copy-start.4
  155.1 110.0 %reduce-scatter.15.cloned.1.call-start = ((), (), s32[]{:S(2)}) async-start(), calls=%async_computation.11 | async-start | bytes 1310720 | tf_op jit(solution)/shard_map/reduce_scatter | solution.py:121
  210.4 4.1 collective-permute-start.2
  211.7 5.2 copy-start.5
  220.7 2.7 copy-start.45
  227.8 0.8 copy-start.25
  228.6 0.7 copy-start.32
  228.6 2.4 copy-start.39
  228.6 2.4 copy-start.6
  233.8 96.5 %reduce-scatter.17.cloned.1.call-start = ((), (), s32[]{:S(2)}) async-start(), calls=%async_computation.12 | async-start | bytes 1310720 | tf_op jit(solution)/shard_map/reduce_scatter | solution.py:121
  265.1 17.7 %copy-start.37 = (bf16[1,128,512]{2,1,0:T(8,128)(2,1)S(1)}, bf16[1,128,512]{2,1,0:T(8,128)(2,1)}, u32[]{:S(2)}) copy-start(bf16[1,128,512]{2,1,0:T(8,128)(2,1)} %copy-done.36) | copy-start | bytes 393220
  267.5 15.2 %copy-start.27 = (bf16[3,32,2048]{2,1,0:T(8,128)(2,1)}, bf16[3,32,2048]{2,1,0:T(8,128)(2,1)S(1)}, u32[]{:S(2)}) copy-start(bf16[3,32,2048]{2,1,0:T(8,128)(2,1)S(1)} %get-tuple-element.340) | copy-start | bytes 1179652
  281.4 5.3 collective-permute-start.3
  282.8 2.6 copy-start.20
  282.8 3.9 copy-start.15
  285.4 3.6 copy-start.7
  285.4 3.5 copy-start.13
  290.9 1.1 copy-start.11
  291.4 1.6 copy-start.46
  298.7 1.9 copy-start.8
  300.6 4.6 copy-start.14
  300.6 4.6 copy-start.22
  303.5 3.5 copy-start.24
  303.5 4.2 copy-start.26
  303.5 240.5 %reduce-scatter.21.cloned.1.call-start = ((), (), s32[]{:S(2)}) async-start(), calls=%async_computation.14 | async-start | bytes 2228224 | tf_op jit(solution)/shard_map/reduce_scatter | solution.py:158
  303.5 3.4 copy-start.40
  315.0 0.9 copy-start.35
  315.1 439.0 %reduce-scatter.19.cloned.1.call-start = ((), (), s32[]{:S(2)}) async-start(), calls=%async_computation.13 | async-start | bytes 2228224 | tf_op jit(solution)/shard_map/reduce_scatter | solution.py:155
  322.5 2.0 copy-start.18
  322.6 641.6 %reduce-scatter.23.cloned.1.call-start = ((), (), s32[]{:S(2)}) async-start(), calls=%async_computation.15 | async-start | bytes 2228224 | tf_op jit(solution)/shard_map/reduce_scatter | solution.py:161
  327.4 2.9 copy-start.12
  327.4 4.0 copy-start.28
Sparse Core Ops, SparseCore 0:
  19.0 33.5 reduce-scatter.8
  85.6 36.8 reduce-scatter.10
  155.3 38.5 reduce-scatter.12
  233.9 31.1 reduce-scatter.14
  303.6 26.6 reduce-scatter.16
  334.5 209.3 reduce-scatter.20
  548.4 205.7 reduce-scatter.18
  758.5 205.6 reduce-scatter.22
where the time goes:
time: 974 us; the launch traced here: 973 us
  waiting for transfers between devices  774 us (79%)
  blocking collectives  56.2 us (6%)
  matrix products  43.6 us (4%)
  local copies, waits for them, and re-layouts  41.6 us (4%)
  other arithmetic  36.2 us (4%)
  between operations  14.8 us (2%)
    reduce_scatter x1, waiting for transfers between devices, shards(): lax.psum_scatter(totals[1].astype(jnp.bfloat16), 'dp', scatter_dimension=...  211 us
    reduce_scatter x1, waiting for transfers between devices, shards(): lax.psum_scatter(totals[0].astype(jnp.bfloat16), 'dp', scatter_dimension=...  209 us
    reduce_scatter x1, waiting for transfers between devices, shards(): lax.psum_scatter(totals[2].astype(jnp.bfloat16), 'dp', scatter_dimension=...  208 us
    reduce_scatter x5, waiting for transfers between devices, shards(): lax.psum_scatter(jnp.dot(d_values, value_w.T, preferred_element_type=jnp....  138 us
    all_gather x4, blocking collectives, shards(): whole_grad = lax.all_gather(d_share, 'tp', axis=0, tiled=True)  56.2 us
  transfers between devices with their start and end apart: 12, of which 11 were waited for; matrix products, arithmetic and copies ran while one was open for 4% of the time, Pallas kernels for 0%

commit v1 on v0

v1 whole, which is shorter than its diff:
```python
import jax
import jax.numpy as jnp
from jax import lax
from jax.sharding import PartitionSpec as P

EPSILON = 1e-06
F32 = jnp.float32
BF16 = jnp.bfloat16


def causal_conv(values, kernel):
    width, length = kernel.shape[0], values.shape[1]
    padded = jnp.pad(values, ((0, 0), (width - 1, 0), (0, 0)))
    total = kernel[0] * values
    for offset in range(1, width):
        begin = width - 1 - offset
        total = total + kernel[offset] * padded[:, begin:begin + length]
    return total


def conv_adjoint(grads, kernel):
    width, length = kernel.shape[0], grads.shape[1]
    padded = jnp.pad(grads, ((0, 0), (0, width - 1), (0, 0)))
    total = kernel[0] * grads
    for offset in range(1, width):
        total = total + kernel[offset] * padded[:, offset:offset + length]
    return total


def dot(a, b, dims):
    return lax.dot_general(a, b, (dims, ((), ())), preferred_element_type=F32)


def shards(activations, upstream_grad, norm_gain, value_weight, gate_weight, out_weight, conv_weight):
    stored = activations[0]
    gain = norm_gain[0]
    value_w, gate_w, out_w, kernel = value_weight[0], gate_weight[0], out_weight[0], conv_weight[0]
    sections = lax.axis_size("pp")
    section = lax.axis_index("pp")
    tp, tp_index = lax.axis_size("tp"), lax.axis_index("tp")
    dp = lax.axis_size("dp")
    micro, length, width = stored.shape
    rows, share = micro * length, length // tp
    channels = value_w.shape[1]
    factor = (micro * length * dp) ** (-0.5)

    floats = stored.astype(F32)
    inv_rms = lax.rsqrt(jnp.mean(floats * floats, axis=-1, keepdims=True) + EPSILON)
    unit = floats * inv_rms
    normed = (unit * gain).astype(BF16).reshape(rows, width)
    values = dot(normed, value_w, ((1,), (0,)))
    gate_logit = dot(normed, gate_w, ((1,), (0,)))
    mixed = causal_conv(values.reshape(micro, length, channels), kernel).reshape(rows, channels)
    sig_mix = jax.nn.sigmoid(mixed)
    act = mixed * sig_mix
    gate = jax.nn.sigmoid(gate_logit)
    hidden = (act * gate).astype(BF16)
    gate_slope = act * gate * (1.0 - gate)
    mix_slope = gate * sig_mix * (1.0 + mixed * (1.0 - sig_mix))
    own = lambda a: lax.dynamic_slice_in_dim(a, tp_index * share, share, 1)
    unit_rows, inv_rows = own(unit), own(inv_rms)

    upstream = upstream_grad
    d_share = jnp.zeros((micro, share, width), BF16)
    grads = tuple(jnp.zeros((width // dp, channels), F32) for _ in range(3))

    def tick(upstream):
        flat = upstream.reshape(rows, width)
        d_hidden = dot(flat, out_w, ((1,), (1,)))
        d_gate = (d_hidden * gate_slope).astype(BF16)
        d_mixed = (d_hidden * mix_slope).reshape(micro, length, channels)
        d_values = conv_adjoint(d_mixed, kernel).astype(BF16).reshape(rows, channels)
        part = dot(d_values, value_w, ((1,), (1,))) + dot(d_gate, gate_w, ((1,), (1,)))
        blocks = part.astype(BF16).reshape(micro, tp, share, width).transpose(1, 0, 2, 3)
        got = lax.all_to_all(blocks, "tp", 0, 0)
        d_unit = jnp.sum(got.astype(F32), axis=0) * gain
        d_rows = own(upstream).astype(F32) + inv_rows * (d_unit - unit_rows * jnp.mean(d_unit * unit_rows, axis=-1, keepdims=True))
        return d_rows.astype(BF16), d_values, d_gate

    def reduced(upstream, d_values, d_gate):
        flat = upstream.reshape(rows, width)
        parts = [dot(normed, d_values, ((0,), (0,))), dot(normed, d_gate, ((0,), (0,))), dot(flat, hidden, ((0,), (0,)))]
        parts = jnp.stack([p.astype(BF16).reshape(dp, width // dp, channels) for p in parts], axis=1)
        got = lax.all_to_all(parts, "dp", 0, 0)
        total = jnp.sum(got.astype(F32), axis=0) * factor
        return total[0], total[1], total[2]

    def finish(grads, saved):
        up, d_values, d_gate, at = saved
        return lax.cond(
            section == at,
            lambda u, v, g, old: reduced(u, v, g),
            lambda u, v, g, old: old,
            up, d_values, d_gate, grads,
        )

    pending = []
    for at in reversed(range(sections)):
        if at < sections - 1:
            pairs = [(i, i ^ (at ^ (at + 1))) for i in range(sections)]
            arrived = lax.cond(
                (section == at) | (section == at + 1),
                lambda s: lax.ppermute(s, "pp", pairs),
                lambda s: s,
                d_share,
            )
            up, d_values, d_gate, done = pending.pop()
            up, arrived = lax.optimization_barrier((up, arrived))
            grads = finish(grads, (up, d_values, d_gate, done))

            def gathered(arrived, upstream):
                got = lax.all_to_all(jnp.broadcast_to(arrived, (tp,) + arrived.shape), "tp", 0, 0)
                return got.transpose(1, 0, 2, 3).reshape(micro, length, width)
        else:
            arrived = d_share

            def gathered(arrived, upstream):
                return upstream

        def active(arrived, upstream, d_share, grads):
            upstream = gathered(arrived, upstream)
            d_share, d_values, d_gate = tick(upstream)
            return upstream, d_share, d_values, d_gate

        def idle(arrived, upstream, d_share, grads):
            empty = jnp.zeros((rows, channels), BF16)
            return upstream, d_share, empty, empty

        upstream, d_share, d_values, d_gate = lax.cond(section == at, active, idle, arrived, upstream, d_share, grads)
        pending.append((upstream, d_values, d_gate, at))
        if at == 0:
            grads = finish(grads, pending.pop())
    return (d_share[None],) + tuple(g[None] for g in grads)


def solution(mesh):
    placed = (
        P("pp", None, "dp", None), P(None, "dp", None), P("pp", None), P("pp", None, "tp"),
        P("pp", None, "tp"), P("pp", "tp", None), P("pp", None, "tp"),
    )
    return jax.shard_map(
        shards, mesh=mesh, in_specs=placed,
        out_specs=(P("pp", None, ("dp", "tp"), None), P("pp", "dp", "tp"), P("pp", "dp", "tp"), P("pp", "dp", "tp")),
        check_vma=False,
    )
```

time: 974 us -> 292 us (0.30)
  waiting for transfers between devices: 774 us -> 20.5 us
  starting transfers between devices: 5.64 us -> 124 us
  blocking collectives: 56.2 us -> 111 us
  matrix products: 43.6 us -> 8.89 us
  other arithmetic: 36.2 us -> 5.6 us
  local copies, waits for them, and re-layouts: 41.6 us -> 20.6 us
  between operations: 14.8 us -> 0.81 us
    reduce_scatter x8 -> x0, waiting for transfers between devices: 766 us -> none  [the longest x1 211 us: shards(): lax.psum_scatter(totals[1].astype(jnp.bfloat16), 'dp', scatter_dimension=...]
    all_to_all x0 -> x1, blocking collectives: none -> 111 us  [reduced(): got = lax.all_to_all(parts, 'dp', 0, 0)]
    ppermute x4 -> x1, starting transfers between devices: 5.13 us -> 113 us  [shards(): lax.ppermute(s, 'pp', pairs)]
    all_gather x4 -> x0, blocking collectives: 56.2 us -> none  [shards(): whole_grad = lax.all_gather(d_share, 'tp', axis=0, tiled=True)]
    dot_general x22 -> x8, matrix products: 43.6 us -> 8.89 us  [dot(): return lax.dot_general(a, b, (dims, ((), ())), preferred_element_type=F32)]
    all_to_all x0 -> x2, waiting for transfers between devices: none -> 19 us  [the longest x1 9.53 us: gathered(): lax.all_to_all(jnp.broadcast_to(arrived, (tp,) + arrived.shape), 'tp', 0, 0)]
    dynamic_update_slice x10 -> x0, other arithmetic: 17.4 us -> none  [the longest x5 11.5 us: shards(): lax.dynamic_update_index_in_dim(saved_upstream, upstream, target, 0)]
    dynamic_update_slice x19 -> x0, local copies, waits for them, and re-layouts: 15.3 us -> none  [the longest x4 5.49 us: shards(): saved_gate = lax.dynamic_update_index_in_dim(saved_gate, d_gate, target, 0)]
  transfers between devices with their start and end apart: 12 -> 3, of which waited for: 11 -> 3; matrix products, arithmetic and copies ran while one was open for 4% -> 0% of each run, Pallas kernels for 0% -> 0%
where the time goes in v1:
time: 292 us
  starting transfers between devices  124 us (42%)
  blocking collectives  111 us (38%)
  local copies, waits for them, and re-layouts  20.6 us (7%)
  waiting for transfers between devices  20.5 us (7%)
  matrix products  8.89 us (3%)
  other arithmetic  5.6 us (2%)
    ppermute x1, starting transfers between devices, shards(): lax.ppermute(s, 'pp', pairs)  113 us
    all_to_all x1, blocking collectives, reduced(): got = lax.all_to_all(parts, 'dp', 0, 0)  111 us
    all_to_all x1, waiting for transfers between devices, gathered(): lax.all_to_all(jnp.broadcast_to(arrived, (tp,) + arrived.shape), 'tp', 0, 0)  9.53 us
    all_to_all x1, waiting for transfers between devices, tick(): got = lax.all_to_all(blocks, 'tp', 0, 0)  9.43 us
    dot_general x8, matrix products, dot(): return lax.dot_general(a, b, (dims, ((), ())), preferred_element_type=F32)  8.89 us
  transfers between devices with their start and end apart: 3, of which 3 were waited for; matrix products, arithmetic and copies ran while one was open for 0% of the time, Pallas kernels for 0%

profile of v1, /device:TPU:8, one launch (start us, length us, event | category | flops | bytes accessed | tf_op | source)
XLA Modules:
  0.0 291.8 jit_solution(6895747383044981993)
XLA Ops:
  0.7 2.4 copy.117
  3.1 0.3 multiply_reduce_fusion.4
  3.4 0.1 fusion.90
  3.5 0.1 constant_dynamic-slice_fusion
  3.6 0.0 copy-start.4
  3.6 0.3 fusion.13
  3.9 0.3 multiply_convert_fusion.4
  4.2 1.0 copy-done.4
  5.2 0.7 fusion.14
  5.9 0.2 multiply_add_fusion
  6.1 0.7 copy-done.8
  6.8 1.0 fusion.28
  7.8 0.0 copy-start
  7.8 0.2 convert_bitcast_fusion
  8.0 0.1 dynamic-slice_multiply_fusion
  8.1 1.4 copy-done
  9.5 0.0 copy-done.13
  9.6 2.2 conditional.11
  9.6 0.7 broadcast.107.clone
  10.3 0.7 broadcast.107
  11.0 0.7 broadcast_in_dim.27
  11.7 1.7 conditional.12
  11.7 1.7 copy.60
  13.4 1.0 copy-done.14
  14.4 0.1 conditional.18
  14.5 0.0 copy-start.29
  14.5 0.0 copy-start.28
  14.5 0.0 copy-start.30
  14.6 0.7 copy-done.29
  15.2 0.1 copy-done.28
  15.3 0.1 copy-done.30
  15.4 0.3 conditional.13
  15.7 1.7 conditional.14
  15.7 1.7 copy.70
  17.4 0.1 conditional.15
  17.4 114.8 %conditional.16 = (bf16[2,32,2048]{2,1,0:T(8,128)(2,1)}) conditional(s32[]{:T(128)} %convert_element_type.205, bf16[2,32,2048]{2,1,0:T(8,128)(2,1)} %get-tuple-element.286, bf16[2,32,2048]{2,1,0:T(8,128)(2,1)} %get-tuple-element.286), branch_computations={%region_17.18_spmd, %region_18.19_spmd} | conditional | bytes 1048624 | solution.py:101
  17.4 113.2 %collective-permute-start.2 = (bf16[2,32,2048]{2,1,0:T(8,128)(2,1)}, bf16[2,32,2048]{2,1,0:T(8,128)(2,1)}, u32[]{:S(2)}, u32[]{:S(2)}) collective-permute-start(bf16[2,32,2048]{2,1,0:T(8,128)(2,1)} %param.11), channel_id=1, source_target_pairs={{0,64},{64,0},{128,192},{192,128},{1,65},{65,1},{129,193},{193,129... | collective-permute-start | bytes 786440 | tf_op jit(solution)/shard_map/cond/branch_1_fun/ppermute | solution.py:103
  130.7 1.5 collective-permute-done.2
  132.2 42.3 %conditional.17 = (bf16[2,128,2048]{2,1,0:T(8,128)(2,1)}, bf16[2,32,2048]{2,1,0:T(8,128)(2,1)}, bf16[256,512]{1,0:T(8,128)(2,1)S(1)}, bf16[256,512]{1,0:T(8,128)(2,1)S(1)}) conditional(s32[]{:T(128)} %convert_element_type.193, (bf16[2,128,2048]{2,1,0:T(8,128)(2,1)}, bf16[2,32,2048]{2,1,0:T(8,128)(2,1)}) %tuple.102, ...), branch_computations={%region_19.20_spmd, %region_20.23_spmd} | conditional | flops 1615331328 | bytes 61122132 | solution.py:129
  132.2 2.0 broadcast_in_dim.30
  134.2 5.7 %all-to-all-start.5 = ((bf16[4,2,32,2048]{3,2,1,0:T(8,128)(2,1)}), bf16[4,2,32,2048]{3,2,1,0:T(8,128)(2,1)}, u32[]{:S(2)}, u32[]{:S(2)}) async-start(bf16[4,2,32,2048]{3,2,1,0:T(8,128)(2,1)} %broadcast_in_dim.30), calls=%async_computation.5 | async-start | bytes 2097152 | tf_op jit(solution)/shard_map/cond/branch_1_fun/all_to_all | solution.py:112
  139.9 9.5 %all-to-all-done.5 = bf16[4,2,32,2048]{3,2,1,0:T(8,128)(2,1)} async-done(((bf16[4,2,32,2048]{3,2,1,0:T(8,128)(2,1)}), bf16[4,2,32,2048]{3,2,1,0:T(8,128)(2,1)}, u32[]{:S(2)}, u32[]{:S(2)}) %all-to-all-start.5) | async-done | bytes 1048608 | tf_op jit(solution)/shard_map/cond/branch_1_fun/all_to_all | solution.py:112
  149.4 2.5 copy.32
  151.9 2.3 multiply_convert_fusion.3
  154.2 0.2 add_convert_fusion.7
  154.5 0.0 copy-start.11
  154.5 0.8 fusion.40
  155.3 0.9 copy-done.11
  156.2 0.7 fusion.9
  156.9 1.1 copy.53
  158.0 4.9 %all-to-all-start.6 = ((bf16[4,2,32,2048]{3,2,1,0:T(8,128)(2,1)}), bf16[4,2,32,2048]{3,2,1,0:T(8,128)(2,1)S(1)}, u32[]{:S(2)}, u32[]{:S(2)}) async-start(bf16[4,2,32,2048]{3,2,1,0:T(8,128)(2,1)} %bitcast.260), calls=%async_computation.6 | async-start | bytes 2097152 | tf_op jit(solution)/shard_map/cond/branch_1_fun/all_to_all | solution.py:75
  162.9 9.4 %all-to-all-done.6 = bf16[4,2,32,2048]{3,2,1,0:T(8,128)(2,1)S(1)} async-done(((bf16[4,2,32,2048]{3,2,1,0:T(8,128)(2,1)}), bf16[4,2,32,2048]{3,2,1,0:T(8,128)(2,1)S(1)}, u32[]{:S(2)}, u32[]{:S(2)}) %all-to-all-start.6) | async-done | bytes 1048608 | tf_op jit(solution)/shard_map/cond/branch_1_fun/all_to_all | solution.py:75
  172.4 0.2 convert_reduce_fusion.3
  172.5 0.1 multiply_reduce_fusion.3
  172.7 1.8 add_convert_fusion.6
  174.5 117.3 %conditional.21 = (f32[1,128,512]{2,1,0:T(8,128)}, f32[1,128,512]{2,1,0:T(8,128)}, f32[1,128,512]{2,1,0:T(8,128)}) conditional(s32[]{:T(128)} %convert_element_type.193, (f32[128,512]{1,0:T(8,128)}, f32[128,512]{1,0:T(8,128)}, f32[128,512]{1,0:T(8,128)}) %get-tuple-element.414, (bf16[256,2048]{1,0:T(8,128)(2,1)S(1)}, ...), branch_computations={%region_32.33_spmd, %region_33.35_spmd} | conditional | flops 1626341376 | bytes 45613080 | solution.py:90
  174.5 0.7 convolution_convert_fusion.11
  175.3 0.7 convolution_convert_fusion.10
  176.0 2.0 convolution_convert_fusion.9
  178.0 0.7 pad_maximum_fusion.3
  178.7 111.2 %all_to_all.47 = bf16[16,3,128,512]{3,2,1,0:T(8,128)(2,1)S(1)} all-to-all(bf16[16,3,128,512]{3,2,1,0:T(8,128)(2,1)S(1)} %pad_maximum_fusion.3), channel_id=1, replica_groups=mesh['pp'=4,'dp'=16,'tp'=4] {'dp'}, dimensions={0} | all-to-all | bytes 12582912 | tf_op jit(solution)/shard_map/cond/branch_1_fun/all_to_all | solution.py:84
  289.8 1.0 convert_reduce_fusion.7
  290.8 0.1 broadcast_multiply_fusion.7
  290.9 0.9 fusion.35
  (34 shorter events, 0.2 us)
Async XLA Ops:
  0.6 2.5 copy-start.12
  0.6 2.9 copy-start.27
  0.7 2.9 copy-start.31
  3.6 1.6 copy-start.4
  5.2 1.6 copy-start.8
  7.8 1.8 copy-start.13
  7.8 1.8 copy-start
  13.4 1.0 copy-start.14
  14.5 0.7 copy-start.29
  14.5 0.8 copy-start.28
  14.5 0.9 copy-start.30
  17.4 114.8 %collective-permute-start.2 = (bf16[2,32,2048]{2,1,0:T(8,128)(2,1)}, bf16[2,32,2048]{2,1,0:T(8,128)(2,1)}, u32[]{:S(2)}, u32[]{:S(2)}) collective-permute-start(bf16[2,32,2048]{2,1,0:T(8,128)(2,1)} %param.11), channel_id=1, source_target_pairs={{0,64},{64,0},{128,192},{192,128},{1,65},{65,1},{129,193},{193,129... | collective-permute-start | bytes 786440 | tf_op jit(solution)/shard_map/cond/branch_1_fun/ppermute | solution.py:103
  134.2 15.2 %all-to-all-start.5 = ((bf16[4,2,32,2048]{3,2,1,0:T(8,128)(2,1)}), bf16[4,2,32,2048]{3,2,1,0:T(8,128)(2,1)}, u32[]{:S(2)}, u32[]{:S(2)}) async-start(bf16[4,2,32,2048]{3,2,1,0:T(8,128)(2,1)} %broadcast_in_dim.30), calls=%async_computation.5 | async-start | bytes 2097152 | tf_op jit(solution)/shard_map/cond/branch_1_fun/all_to_all | solution.py:112
  149.4 2.5 copy-start.3
  151.9 2.5 copy-start.7
  154.2 1.1 copy-start.25
  154.5 0.8 copy-start.19
  154.5 1.7 copy-start.11
  158.0 14.4 %all-to-all-start.6 = ((bf16[4,2,32,2048]{3,2,1,0:T(8,128)(2,1)}), bf16[4,2,32,2048]{3,2,1,0:T(8,128)(2,1)S(1)}, u32[]{:S(2)}, u32[]{:S(2)}) async-start(bf16[4,2,32,2048]{3,2,1,0:T(8,128)(2,1)} %bitcast.260), calls=%async_computation.6 | async-start | bytes 2097152 | tf_op jit(solution)/shard_map/cond/branch_1_fun/all_to_all | solution.py:75
  162.9 11.6 %copy-start.20 = (bf16[2,128,512]{2,1,0:T(8,128)(2,1)S(1)}, bf16[2,128,512]{2,1,0:T(8,128)(2,1)}, u32[]{:S(2)}) copy-start(bf16[2,128,512]{2,1,0:T(8,128)(2,1)} %copy-done.19) | copy-start | bytes 786436 | tf_op jit(solution)/shard_map/cond
  162.9 11.6 %copy-start.26 = (bf16[256,512]{1,0:T(8,128)(2,1)S(1)}, bf16[256,512]{1,0:T(8,128)(2,1)}, u32[]{:S(2)}) copy-start(bf16[256,512]{1,0:T(8,128)(2,1)} %copy-done.25) | copy-start | bytes 786436 | tf_op jit(solution)/shard_map/cond
